TPU v7x, 32 devices: a whole 2x2x4 slice. The times are simulated.
32 devices in a mesh: group: 8 (over z, core), lane: 4 (over y, x).
Axes of the slice: x: 2, y: 2, z: 4, core: 2. Of those that a mesh axis runs over, the one named last changes fastest.
Arguments:
- node_feat: float32 [16384, 128], P(('group', 'lane')), may hold values from -6 to 6
- hub_feat: float32 [128, 128], P('lane'), may hold values from -6 to 6
- edge_feat: float32 [65536, 128], P(('group', 'lane')), may hold values from -6 to 6
- src_slot: int32 [65536], P(('group', 'lane')), may hold values from 0 to 831, as said below
- dst_slot: int32 [65536], P(('group', 'lane')), may hold values from 0 to 831, as said below
- sign_bit: int32 [65536], P(('group', 'lane')), may hold values from 0 to 1
- send_rows: int32 [128, 48], P(('group', 'lane')), may hold values from -1 to 511, as said below
- w_edge_in: float32 [384, 512], replicated, may hold values from -0.3125 to 0.3125
- b_edge_in: float32 [512], replicated, may hold values from -3 to 3
- w_edge_out: float32 [512, 128], replicated, may hold values from -0.25 to 0.25
- b_edge_out: float32 [128], replicated, may hold values from -3 to 3
- w_node_in: float32 [256, 512], replicated, may hold values from -0.375 to 0.375
- b_node_in: float32 [512], replicated, may hold values from -3 to 3
- w_node_out: float32 [512, 128], replicated, may hold values from -0.25 to 0.25
- b_node_out: float32 [128], replicated, may hold values from -3 to 3
Outputs:
- node_out: float32 [16384, 128], P(('group', 'lane'))
- hub_out: float32 [128, 128], P('lane')
Inputs may be any that keep to these rules, and one draw needn't show every extreme that they name: `send_rows`: row d * 4 + p lists local rows of device d's vertices mirrored on lane p of d's group: distinct rows, then -1 to the end. Lists hold 0 to 48 rows, and one list of every device holds 48. `src_slot`: mirror rows named by an edge are live: row 512 + p * 48 + c with c below the length of lane p's list to this device's lane. `dst_slot`: as for src_slot.
All inputs are finite; a program needn't handle non-finite values.
Results may differ from a plain program's by a relative error of at most 0.00005.
Values sent between devices are 32-bit elements; how exact they have to be, the bound alone decides.
A program may use at most 64 MiB of HBM per device.

v0:
```python
import functools
import math

import jax
import jax.numpy as jnp
from jax import lax
from jax.experimental import pallas as pl
from jax.experimental.pallas import tpu as pltpu
from jax.sharding import PartitionSpec as P

MESH = pl.DeviceIdType.MESH
F32, BF16 = jnp.float32, jnp.bfloat16


def split(x):
    hi = x.astype(BF16)
    return hi, (x - hi.astype(F32)).astype(BF16)


def dot(a, b):
    return jnp.dot(a, b, preferred_element_type=F32)


def silu(v):
    return v / (1.0 + jnp.exp(-v))


def column(row):
    return jnp.transpose(jnp.broadcast_to(row, (128, row.shape[1])))


def store_weights(w_ref, stack_ref, low_ref):
    for b in range(w_ref.shape[0] // 128):
        hi, lo = split(w_ref[128 * b : 128 * (b + 1), :])
        stack_ref[256 * b : 256 * b + 128, :] = hi
        stack_ref[256 * b + 128 : 256 * b + 256, :] = hi
        low_ref[128 * b : 128 * (b + 1), :] = lo


def store_out_weights(w_ref, pair_ref):
    hi, lo = split(w_ref[...])
    pair_ref[:, :128] = hi
    pair_ref[:, 128:] = lo


def out_layer(hidden, pair_ref):
    hi, lo = split(hidden)
    both = dot(hi, pair_ref[...])
    return both[:, :128] + both[:, 128:] + dot(lo, pair_ref[:, :128])


def kernel(
    sizes,
    node, hub, edge, src, dst, sgn, rows, w1, b1, w2, b2, w3, b3, w4, b4,
    node_out, hub_out,
    w1s, w1l, w2p, w3s, w3l, w4p,
    table, outbuf, mir, hubs, oh_s, oh_d, oh_t, sums, dacc, res, back, huba, hubb, hubsend,
    m_send, m_recv, h_send, h_recv, r_send, r_recv, a_send, a_recv, g_send, g_recv,
):
    L, G, V, CAP, H, HS, E, EB, T, TP = sizes
    LC = L * CAP
    lane = lax.axis_index("lane")
    group = lax.axis_index("group")
    barrier = pltpu.get_barrier_semaphore()
    lanes = [lax.rem(lane + k, L) for k in range(1, L)]
    groups = [lax.rem(group + k, G) for k in range(1, G)]
    for p in lanes:
        pl.semaphore_signal(barrier, inc=1, device_id=(group, p), device_id_type=MESH)
    for q in groups:
        pl.semaphore_signal(barrier, inc=1, device_id=(q, lane), device_id_type=MESH)

    hi, lo = split(node[...])
    table[:V, :128] = hi
    table[:V, 128:] = lo
    if TP > T:
        table[T:, :] = jnp.zeros((TP - T, 256), BF16)
    LCP = -(-LC // 128) * 128
    pieces = [rows[p : p + 1, :] for p in range(L)]
    if LCP > LC:
        pieces.append(jnp.full((1, LCP - LC), -1, jnp.int32))
    flat_rows = jnp.concatenate(pieces, axis=1)
    lane_iota = lax.broadcasted_iota(jnp.int32, (128, 128), 1)
    flat_col = column(flat_rows)[:LC]
    lane_iota_lc = lax.broadcasted_iota(jnp.int32, (LC, 128), 1)
    send_hot = jnp.concatenate(
        [jnp.where(flat_col == lane_iota_lc + 128 * k, 1.0, 0.0).astype(BF16) for k in range(V // 128)], axis=1
    )
    both = dot(send_hot, table[:V, :])
    outbuf[...] = both[:, :128] + both[:, 128:]

    pl.semaphore_wait(barrier, L - 1 + G - 1)

    def remote(src_ref, dst_ref, s_sem, r_sem, g, l):
        return pltpu.make_async_remote_copy(
            src_ref=src_ref, dst_ref=dst_ref, send_sem=s_sem, recv_sem=r_sem,
            device_id=(g, l), device_id_type=MESH,
        )

    def part(p, n, start=0):
        return pl.ds(pl.multiple_of(start + p * n, 16), n)

    sends = []
    for p in lanes:
        c = remote(outbuf.at[part(p, CAP)], mir.at[part(lane, CAP)], m_send.at[p], m_recv.at[lane], group, p)
        c.start()
        sends.append(c)
        c = remote(hub, hubs.at[part(lane, HS)], h_send.at[p], h_recv.at[lane], group, p)
        c.start()
        sends.append(c)
    mir[part(lane, CAP), :] = outbuf[part(lane, CAP), :]
    hubs[part(lane, HS), :] = hub[...]

    store_weights(w1, w1s, w1l)
    store_out_weights(w2, w2p)
    store_weights(w3, w3s, w3l)
    store_out_weights(w4, w4p)
    sums[...] = jnp.zeros(sums.shape, F32)
    dacc[...] = jnp.zeros(dacc.shape, F32)

    for p in lanes:
        remote(outbuf.at[part(p, CAP)], mir.at[part(p, CAP)], m_send.at[p], m_recv.at[p], group, p).wait_recv()
        remote(hub, hubs.at[part(p, HS)], h_send.at[p], h_recv.at[p], group, p).wait_recv()
    hi, lo = split(mir[...])
    table[V : V + LC, :128] = hi
    table[V : V + LC, 128:] = lo
    hi, lo = split(hubs[...])
    table[V + LC : T, :128] = hi
    table[V + LC : T, 128:] = lo

    NR = EB // 128
    sub_iota = lax.broadcasted_iota(jnp.int32, (T, 128), 0)

    def edge_block(i, carry):
        signs = []
        for j in range(NR):
            at = pl.ds(i * NR + j, 1)
            row = slice(128 * j, 128 * (j + 1))
            s_col = column(src[at, :])
            d_row = dst[at, :]
            d_col = column(d_row)
            for k in range(TP // 128):
                ids = lane_iota + 128 * k
                cols = slice(128 * k, 128 * (k + 1))
                oh_s[row, cols] = jnp.where(s_col == ids, 1.0, 0.0).astype(BF16)
                oh_d[row, cols] = jnp.where(d_col == ids, 1.0, 0.0).astype(BF16)
            hot = jnp.where(sub_iota == d_row, 1.0, 0.0)
            oh_t[:, row] = hot.astype(BF16)
            dacc[...] += hot
            signs.append((2 * column(sgn[at, :]) - 1).astype(F32))
        xs = dot(oh_s[...], table[...]).astype(BF16)
        xd = dot(oh_d[...], table[...]).astype(BF16)
        eh, el = split(edge[pl.ds(pl.multiple_of(i * EB, EB), EB), :])
        pre = dot(jnp.concatenate([xs, xd, eh, el], axis=1), w1s[...])
        pre = pre + dot(jnp.concatenate([xs[:, :128], xd[:, :128], eh], axis=1), w1l[...])
        h = silu(pre + b1[...])
        m = (out_layer(h, w2p) + b2[...]) * jnp.concatenate(signs, axis=0)
        mh, ml = split(m)
        sums[...] += dot(oh_t[...], jnp.concatenate([mh, ml], axis=1))
        return carry

    lax.fori_loop(0, E // EB, edge_block, 0)

    res[:, :128] = sums[:, :128] + sums[:, 128:]
    res[:, 128:] = dot(dacc[...].astype(BF16), jnp.ones((128, 128), BF16))
    for p in lanes:
        c = remote(res.at[part(p, HS, V + LC)], huba.at[part(lane, HS)], a_send.at[p], a_recv.at[lane], group, p)
        c.start()
        sends.append(c)
    for p in lanes:
        c = remote(res.at[part(p, CAP, V)], back.at[part(lane, CAP)], r_send.at[p], r_recv.at[lane], group, p)
        c.start()
        sends.append(c)
    huba[part(lane, HS), :] = res[part(lane, HS, V + LC), :]
    back[part(lane, CAP), :] = res[part(lane, CAP, V), :]

    for p in lanes:
        remote(res.at[part(p, HS)], huba.at[part(p, HS)], a_send.at[p], a_recv.at[p], group, p).wait_recv()
    total = huba[:HS, :]
    for p in range(1, L):
        total = total + huba[HS * p : HS * (p + 1), :]
    deg = jnp.concatenate([total[:, 128:], jnp.zeros((128 - HS, 128), F32)], axis=0)
    hubsend[:HS, :] = total[:, :128]
    hubsend[HS:, :] = jnp.transpose(deg)[:8, :]
    for q in groups:
        c = remote(hubsend, hubb.at[group], g_send.at[q], g_recv.at[group], q, lane)
        c.start()
        sends.append(c)
    hubb[group] = hubsend[...]

    for p in lanes:
        remote(res.at[part(p, CAP)], back.at[part(p, CAP)], r_send.at[p], r_recv.at[p], group, p).wait_recv()
    v_iota = lax.broadcasted_iota(jnp.int32, (V, LC), 0)
    back_hot = jnp.where(v_iota == flat_rows[:, :LC], 1.0, 0.0).astype(BF16)
    sh, sl = split(back[:, :128])
    dh, dl = split(back[:, 128:])
    got = dot(back_hot, jnp.concatenate([sh, sl], axis=1))
    got_deg = dot(back_hot, jnp.concatenate([dh, dl], axis=1))

    def update(x, summed, degree):
        xh, xl = split(x)
        mh, ml = split(summed / jnp.maximum(degree, 1.0))
        pre = dot(jnp.concatenate([xh, xl, mh, ml], axis=1), w3s[...])
        pre = pre + dot(jnp.concatenate([xh, mh], axis=1), w3l[...])
        return x + out_layer(silu(pre + b3[...]), w4p) + b4[...]

    node_out[...] = update(
        node[...],
        res[:V, :128] + got[:, :128] + got[:, 128:],
        res[:V, 128:] + got_deg[:, :128] + got_deg[:, 128:],
    )

    for q in groups:
        remote(hubsend, hubb.at[q], g_send.at[q], g_recv.at[q], q, lane).wait_recv()
    whole = hubb[0]
    for q in range(1, G):
        whole = whole + hubb[q]
    hub_out[...] = update(hub[...], whole[:HS, :], column(whole[HS : HS + 1, :])[:HS])
    for c in sends:
        c.wait_send()


def per_device(node, hub, edge, src, dst, sgn, rows, w1, b1, w2, b2, w3, b3, w4, b4):
    L, G = lax.axis_size("lane"), lax.axis_size("group")
    V, D = node.shape
    CAP = rows.shape[1]
    HS = hub.shape[0]
    H = HS * L
    E = edge.shape[0]
    HID = w1.shape[1]
    EB = math.gcd(512, E)
    T = V + L * CAP + H
    TP = -(-T // 128) * 128
    sizes = (L, G, V, CAP, H, HS, E, EB, T, TP)
    dma = pltpu.SemaphoreType.DMA
    vmem = pl.BlockSpec(memory_space=pltpu.VMEM)
    return pl.pallas_call(
        functools.partial(kernel, sizes),
        out_shape=(jax.ShapeDtypeStruct((V, D), F32), jax.ShapeDtypeStruct((HS, D), F32)),
        in_specs=[vmem] * 15,
        out_specs=(vmem, vmem),
        scratch_shapes=[
            pltpu.VMEM((6 * D, HID), BF16),
            pltpu.VMEM((3 * D, HID), BF16),
            pltpu.VMEM((HID, 2 * D), BF16),
            pltpu.VMEM((4 * D, HID), BF16),
            pltpu.VMEM((2 * D, HID), BF16),
            pltpu.VMEM((HID, 2 * D), BF16),
            pltpu.VMEM((TP, 2 * D), BF16),
            pltpu.VMEM((L * CAP, D), F32),
            pltpu.VMEM((L * CAP, D), F32),
            pltpu.VMEM((H, D), F32),
            pltpu.VMEM((EB, TP), BF16),
            pltpu.VMEM((EB, TP), BF16),
            pltpu.VMEM((T, EB), BF16),
            pltpu.VMEM((T, 2 * D), F32),
            pltpu.VMEM((T, 128), F32),
            pltpu.VMEM((T, 2 * D), F32),
            pltpu.VMEM((L * CAP, 2 * D), F32),
            pltpu.VMEM((H, 2 * D), F32),
            pltpu.VMEM((G, HS + 8, D), F32),
            pltpu.VMEM((HS + 8, D), F32),
        ]
        + [dma((L,))] * 8
        + [dma((G,))] * 2,
        compiler_params=pltpu.CompilerParams(
            collective_id=0, has_side_effects=True, vmem_limit_bytes=48 * 2**20
        ),
    )(
        node, hub, edge, src.reshape(-1, 128), dst.reshape(-1, 128), sgn.reshape(-1, 128), rows,
        w1, b1.reshape(1, -1), w2, b2.reshape(1, -1), w3, b3.reshape(1, -1), w4, b4.reshape(1, -1),
    )


def solution(mesh):
    rows = P(("group", "lane"), None)
    flat = P(("group", "lane"))
    return jax.shard_map(
        per_device,
        mesh=mesh,
        in_specs=(rows, P("lane", None), rows, flat, flat, flat, rows) + (P(),) * 8,
        out_specs=(rows, P("lane", None)),
        check_vma=False,
    )
```

profile of v0, /device:TPU:0, one launch (start us, length us, event | category | flops | bytes accessed | tf_op | source)
XLA Modules:
  0.0 40.4 jit_solution(4912866484679329843)
XLA Ops:
  0.6 0.0 copy-start.7
  0.6 0.0 copy-start.11
  0.7 0.0 copy-start.10
  0.7 0.0 copy-start.13
  0.7 0.0 copy-start.14
  0.7 0.6 %copy-done.7 = s32[2048]{0:T(1024)S(1)} copy-done((s32[2048]{0:T(1024)S(1)}, s32[2048]{0:T(1024)}, u32[]{:S(2)}) %copy-start.7) | copy-done | bytes 8216
  1.3 0.0 copy-done.11
  1.3 0.0 copy-done.10
  1.4 0.0 copy-done.13
  1.4 0.0 copy-done.14
  1.4 0.0 copy-start
  1.4 1.2 %copy-done = f32[2048,128]{1,0:T(8,128)S(1)} copy-done((f32[2048,128]{1,0:T(8,128)S(1)}, f32[2048,128]{1,0:T(8,128)}, u32[]{:S(2)}) %copy-start) | copy-done | bytes 1048600
  2.6 0.0 copy-start.1
  2.6 1.1 %copy-done.1 = f32[384,512]{1,0:T(8,128)S(1)} copy-done((f32[384,512]{1,0:T(8,128)S(1)}, f32[384,512]{1,0:T(8,128)}, u32[]{:S(2)}) %copy-start.1) | copy-done | bytes 786456
  3.7 0.0 copy-start.2
  3.7 1.0 %copy-done.2 = f32[256,512]{1,0:T(8,128)S(1)} copy-done((f32[256,512]{1,0:T(8,128)S(1)}, f32[256,512]{1,0:T(8,128)}, u32[]{:S(2)}) %copy-start.2) | copy-done | bytes 524312
  4.8 0.0 copy-start.3
  4.8 0.9 %copy-done.3 = f32[512,128]{1,0:T(8,128)S(1)} copy-done((f32[512,128]{1,0:T(8,128)S(1)}, f32[512,128]{1,0:T(8,128)}, u32[]{:S(2)}) %copy-start.3) | copy-done | bytes 262168
  5.7 0.0 copy-start.4
  5.7 0.9 %copy-done.4 = f32[512,128]{1,0:T(8,128)S(1)} copy-done((f32[512,128]{1,0:T(8,128)S(1)}, f32[512,128]{1,0:T(8,128)}, u32[]{:S(2)}) %copy-start.4) | copy-done | bytes 262168
  6.7 0.0 copy-start.5
  6.7 0.9 %copy-done.5 = f32[512,128]{1,0:T(8,128)S(1)} copy-done((f32[512,128]{1,0:T(8,128)S(1)}, f32[512,128]{1,0:T(8,128)}, u32[]{:S(2)}) %copy-start.5) | copy-done | bytes 262168
  7.6 0.0 copy-start.6
  7.6 0.7 %copy-done.6 = f32[32,128]{1,0:T(8,128)S(1)} copy-done((f32[32,128]{1,0:T(8,128)S(1)}, f32[32,128]{1,0:T(8,128)}, u32[]{:S(2)}) %copy-start.6) | copy-done | bytes 16408
  8.3 0.0 copy-start.8
  8.3 0.7 %copy-done.8 = s32[2048]{0:T(1024)S(1)} copy-done((s32[2048]{0:T(1024)S(1)}, s32[2048]{0:T(1024)}, u32[]{:S(2)}) %copy-start.8) | copy-done | bytes 8216
  9.0 0.0 copy-start.9
  9.0 0.7 %copy-done.9 = s32[2048]{0:T(1024)S(1)} copy-done((s32[2048]{0:T(1024)S(1)}, s32[2048]{0:T(1024)}, u32[]{:S(2)}) %copy-start.9) | copy-done | bytes 8216
  9.7 0.0 copy-start.12
  9.7 0.7 %copy-done.12 = f32[512]{0:T(512)S(1)} copy-done((f32[512]{0:T(512)S(1)}, f32[512]{0:T(512)}, u32[]{:S(2)}) %copy-start.12) | copy-done | bytes 2072
  10.4 28.6 %shard_map.158 = (f32[512,128]{1,0:T(8,128)S(1)}, f32[32,128]{1,0:T(8,128)S(1)}) custom-call(f32[512,128]{1,0:T(8,128)S(1)} %copy-done.3, f32[32,128]{1,0:T(8,128)S(1)} %copy-done.6, f32[2048,128]{1,0:T(8,128)S(1)} %copy-done, s32[16,128]{1,0:T(8,128)S(1)} %bitcast.7, s32[16,128]{1,0:T(8,128)S(1)} %bitcast.8, s32[16,128]{1,0:T(8,128)S(1)} %bitcast.9, ...), custom_call_target="tpu_custom_call" | custom-call | tf_op jit(solution)/shard_map/pallas_call | solution.py:236
  39.0 0.7 %copy.19 = f32[512,128]{1,0:T(8,128)} copy(f32[512,128]{1,0:T(8,128)S(1)} %get-tuple-element.4) | data formatting | bytes 524288
  39.7 0.6 %copy.20 = f32[32,128]{1,0:T(8,128)} copy(f32[32,128]{1,0:T(8,128)S(1)} %get-tuple-element.5) | data formatting | bytes 32768
Async XLA Ops:
  0.6 0.7 %copy-start.7 = (s32[2048]{0:T(1024)S(1)}, s32[2048]{0:T(1024)}, u32[]{:S(2)}) copy-start(s32[2048]{0:T(1024)} %param.18) | copy-start | bytes 24580
  0.6 0.7 %copy-start.11 = (f32[512]{0:T(512)S(1)}, f32[512]{0:T(512)}, u32[]{:S(2)}) copy-start(f32[512]{0:T(512)} %param.23) | copy-start | bytes 6148
  0.7 0.7 %copy-start.10 = (s32[4,48]{1,0:T(4,128)S(1)}, s32[4,48]{1,0:T(4,128)}, u32[]{:S(2)}) copy-start(s32[4,48]{1,0:T(4,128)} %rows.1) | copy-start | bytes 2308
  0.7 0.7 %copy-start.13 = (f32[128]{0:T(128)S(1)}, f32[128]{0:T(128)}, u32[]{:S(2)}) copy-start(f32[128]{0:T(128)} %param.25) | copy-start | bytes 1540
  0.7 0.7 %copy-start.14 = (f32[128]{0:T(128)S(1)}, f32[128]{0:T(128)}, u32[]{:S(2)}) copy-start(f32[128]{0:T(128)} %param.29) | copy-start | bytes 1540
  1.4 1.2 %copy-start = (f32[2048,128]{1,0:T(8,128)S(1)}, f32[2048,128]{1,0:T(8,128)}, u32[]{:S(2)}) copy-start(f32[2048,128]{1,0:T(8,128)} %edge.1) | copy-start | bytes 3145732
  2.6 1.1 %copy-start.1 = (f32[384,512]{1,0:T(8,128)S(1)}, f32[384,512]{1,0:T(8,128)}, u32[]{:S(2)}) copy-start(f32[384,512]{1,0:T(8,128)} %w1.1) | copy-start | bytes 2359300
  3.7 1.0 %copy-start.2 = (f32[256,512]{1,0:T(8,128)S(1)}, f32[256,512]{1,0:T(8,128)}, u32[]{:S(2)}) copy-start(f32[256,512]{1,0:T(8,128)} %w3.1) | copy-start | bytes 1572868
  4.8 0.9 %copy-start.3 = (f32[512,128]{1,0:T(8,128)S(1)}, f32[512,128]{1,0:T(8,128)}, u32[]{:S(2)}) copy-start(f32[512,128]{1,0:T(8,128)} %node.1) | copy-start | bytes 786436
  5.7 0.9 %copy-start.4 = (f32[512,128]{1,0:T(8,128)S(1)}, f32[512,128]{1,0:T(8,128)}, u32[]{:S(2)}) copy-start(f32[512,128]{1,0:T(8,128)} %w2.1) | copy-start | bytes 786436
  6.7 0.9 %copy-start.5 = (f32[512,128]{1,0:T(8,128)S(1)}, f32[512,128]{1,0:T(8,128)}, u32[]{:S(2)}) copy-start(f32[512,128]{1,0:T(8,128)} %w4.1) | copy-start | bytes 786436
  7.6 0.7 %copy-start.6 = (f32[32,128]{1,0:T(8,128)S(1)}, f32[32,128]{1,0:T(8,128)}, u32[]{:S(2)}) copy-start(f32[32,128]{1,0:T(8,128)} %hub.1) | copy-start | bytes 49156
  8.3 0.7 %copy-start.8 = (s32[2048]{0:T(1024)S(1)}, s32[2048]{0:T(1024)}, u32[]{:S(2)}) copy-start(s32[2048]{0:T(1024)} %param.19) | copy-start | bytes 24580
  9.0 0.7 %copy-start.9 = (s32[2048]{0:T(1024)S(1)}, s32[2048]{0:T(1024)}, u32[]{:S(2)}) copy-start(s32[2048]{0:T(1024)} %param.20) | copy-start | bytes 24580
  9.7 0.7 %copy-start.12 = (f32[512]{0:T(512)S(1)}, f32[512]{0:T(512)}, u32[]{:S(2)}) copy-start(f32[512]{0:T(512)} %param.27) | copy-start | bytes 6148
where the time goes:
time: 40.9 us; the launch traced here: 40.4 us
  Pallas kernels  28.6 us (70%)
  local copies, waits for them, and re-layouts  11 us (27%)
  between operations  0.7 us (2%)
    pallas_call x1, Pallas kernels, per_device(): pl.pallas_call(functools.partial(kernel, sizes), out_shape=(jax.ShapeDtyp...  28.6 us
    unnamed x32, local copies, waits for them, and re-layouts  11 us

commit v1 on v0

--- a/solution.py
+++ b/solution.py
@@ -22,7 +22,7 @@
 
 
 def silu(v):
-    return v / (1.0 + jnp.exp(-v))
+    return v + v * jnp.tanh(v)
 
 
 def column(row):
@@ -31,7 +31,7 @@
 
 def store_weights(w_ref, stack_ref, low_ref):
     for b in range(w_ref.shape[0] // 128):
-        hi, lo = split(w_ref[128 * b : 128 * (b + 1), :])
+        hi, lo = split(0.5 * w_ref[128 * b : 128 * (b + 1), :])
         stack_ref[256 * b : 256 * b + 128, :] = hi
         stack_ref[256 * b + 128 : 256 * b + 256, :] = hi
         low_ref[128 * b : 128 * (b + 1), :] = lo
@@ -51,8 +51,9 @@
 
 def kernel(
     sizes,
-    node, hub, edge, src, dst, sgn, rows, w1, b1, w2, b2, w3, b3, w4, b4,
+    node_h, hub_h, edge_h, src_h, dst_h, sgn_h, rows_h, w1_h, b1_h, w2_h, b2_h, w3_h, b3_h, w4_h, b4_h,
     node_out, hub_out,
+    node, hub, edge, src, dst, sgn, rows, w1, b1, w2, b2, w3, b3, w4, b4, in_sem,
     w1s, w1l, w2p, w3s, w3l, w4p,
     table, outbuf, mir, hubs, oh_s, oh_d, oh_t, sums, dacc, res, back, huba, hubb, hubsend,
     m_send, m_recv, h_send, h_recv, r_send, r_recv, a_send, a_recv, g_send, g_recv,
@@ -68,6 +69,14 @@
         pl.semaphore_signal(barrier, inc=1, device_id=(group, p), device_id_type=MESH)
     for q in groups:
         pl.semaphore_signal(barrier, inc=1, device_id=(q, lane), device_id_type=MESH)
+
+    far = (rows_h, node_h, hub_h, src_h, dst_h, w1_h, edge_h, w2_h, sgn_h, b1_h, b2_h, w3_h, w4_h, b3_h, b4_h)
+    near = (rows, node, hub, src, dst, w1, edge, w2, sgn, b1, b2, w3, w4, b3, b4)
+    loads = [pltpu.make_async_copy(f, n, in_sem.at[i]) for i, (f, n) in enumerate(zip(far, near))]
+    for c in loads:
+        c.start()
+    for c in loads[:3]:
+        c.wait()
 
     hi, lo = split(node[...])
     table[:V, :128] = hi
@@ -110,12 +119,14 @@
     mir[part(lane, CAP), :] = outbuf[part(lane, CAP), :]
     hubs[part(lane, HS), :] = hub[...]
 
+    for c in loads[3:]:
+        c.wait()
     store_weights(w1, w1s, w1l)
     store_out_weights(w2, w2p)
     store_weights(w3, w3s, w3l)
     store_out_weights(w4, w4p)
     sums[...] = jnp.zeros(sums.shape, F32)
-    dacc[...] = jnp.zeros(dacc.shape, F32)
+    dacc[...] = jnp.zeros(dacc.shape, BF16)
 
     for p in lanes:
         remote(outbuf.at[part(p, CAP)], mir.at[part(p, CAP)], m_send.at[p], m_recv.at[p], group, p).wait_recv()
@@ -128,31 +139,42 @@
     table[V + LC : T, 128:] = lo
 
     NR = EB // 128
-    sub_iota = lax.broadcasted_iota(jnp.int32, (T, 128), 0)
+    lane_id = lane_iota.astype(F32).astype(BF16)
+    sub_id = lax.broadcasted_iota(jnp.int32, (128, 128), 0).astype(F32).astype(BF16)
+    one, zero = jnp.ones((128, 128), BF16), jnp.zeros((128, 128), BF16)
+
+    def digits(ids):
+        high = ids >> 7
+        return (ids & 127).astype(F32).astype(BF16), high.astype(F32).astype(BF16)
 
     def edge_block(i, carry):
         signs = []
         for j in range(NR):
             at = pl.ds(i * NR + j, 1)
             row = slice(128 * j, 128 * (j + 1))
-            s_col = column(src[at, :])
             d_row = dst[at, :]
-            d_col = column(d_row)
+            s_low, s_high = digits(column(src[at, :]))
+            d_low, d_high = digits(column(d_row))
+            r_low, r_high = digits(jnp.broadcast_to(d_row, (128, 128)))
+            s_hot = jnp.where(s_low == lane_id, one, zero)
+            d_hot = jnp.where(d_low == lane_id, one, zero)
+            r_hot = jnp.where(r_low == sub_id, one, zero)
             for k in range(TP // 128):
-                ids = lane_iota + 128 * k
                 cols = slice(128 * k, 128 * (k + 1))
-                oh_s[row, cols] = jnp.where(s_col == ids, 1.0, 0.0).astype(BF16)
-                oh_d[row, cols] = jnp.where(d_col == ids, 1.0, 0.0).astype(BF16)
-            hot = jnp.where(sub_iota == d_row, 1.0, 0.0)
-            oh_t[:, row] = hot.astype(BF16)
-            dacc[...] += hot
+                k16 = jnp.asarray(k, BF16)
+                oh_s[row, cols] = jnp.where(s_high == k16, s_hot, zero)
+                oh_d[row, cols] = jnp.where(d_high == k16, d_hot, zero)
+                n = min(128, T - 128 * k)
+                hot = jnp.where(r_high == k16, r_hot, zero)[:n]
+                oh_t[128 * k : 128 * k + n, row] = hot
+                dacc[128 * k : 128 * k + n, :] += hot
             signs.append((2 * column(sgn[at, :]) - 1).astype(F32))
         xs = dot(oh_s[...], table[...]).astype(BF16)
         xd = dot(oh_d[...], table[...]).astype(BF16)
         eh, el = split(edge[pl.ds(pl.multiple_of(i * EB, EB), EB), :])
         pre = dot(jnp.concatenate([xs, xd, eh, el], axis=1), w1s[...])
         pre = pre + dot(jnp.concatenate([xs[:, :128], xd[:, :128], eh], axis=1), w1l[...])
-        h = silu(pre + b1[...])
+        h = silu(pre + 0.5 * b1[...])
         m = (out_layer(h, w2p) + b2[...]) * jnp.concatenate(signs, axis=0)
         mh, ml = split(m)
         sums[...] += dot(oh_t[...], jnp.concatenate([mh, ml], axis=1))
@@ -161,7 +183,7 @@
     lax.fori_loop(0, E // EB, edge_block, 0)
 
     res[:, :128] = sums[:, :128] + sums[:, 128:]
-    res[:, 128:] = dot(dacc[...].astype(BF16), jnp.ones((128, 128), BF16))
+    res[:, 128:] = dot(dacc[...], jnp.ones((128, 128), BF16))
     for p in lanes:
         c = remote(res.at[part(p, HS, V + LC)], huba.at[part(lane, HS)], a_send.at[p], a_recv.at[lane], group, p)
         c.start()
@@ -201,7 +223,7 @@
         mh, ml = split(summed / jnp.maximum(degree, 1.0))
         pre = dot(jnp.concatenate([xh, xl, mh, ml], axis=1), w3s[...])
         pre = pre + dot(jnp.concatenate([xh, mh], axis=1), w3l[...])
-        return x + out_layer(silu(pre + b3[...]), w4p) + b4[...]
+        return x + out_layer(silu(pre + 0.5 * b3[...]), w4p) + b4[...]
 
     node_out[...] = update(
         node[...],
@@ -231,14 +253,21 @@
     T = V + L * CAP + H
     TP = -(-T // 128) * 128
     sizes = (L, G, V, CAP, H, HS, E, EB, T, TP)
+    assert E <= 256 * 128
     dma = pltpu.SemaphoreType.DMA
     vmem = pl.BlockSpec(memory_space=pltpu.VMEM)
+    args = (
+        node, hub, edge, src.reshape(-1, 128), dst.reshape(-1, 128), sgn.reshape(-1, 128), rows,
+        w1, b1.reshape(1, -1), w2, b2.reshape(1, -1), w3, b3.reshape(1, -1), w4, b4.reshape(1, -1),
+    )
     return pl.pallas_call(
         functools.partial(kernel, sizes),
         out_shape=(jax.ShapeDtypeStruct((V, D), F32), jax.ShapeDtypeStruct((HS, D), F32)),
-        in_specs=[vmem] * 15,
+        in_specs=[pl.BlockSpec(memory_space=pltpu.HBM)] * 15,
         out_specs=(vmem, vmem),
-        scratch_shapes=[
+        scratch_shapes=[pltpu.VMEM(a.shape, a.dtype) for a in args]
+        + [dma((15,))]
+        + [
             pltpu.VMEM((6 * D, HID), BF16),
             pltpu.VMEM((3 * D, HID), BF16),
             pltpu.VMEM((HID, 2 * D), BF16),
@@ -253,7 +282,7 @@
             pltpu.VMEM((EB, TP), BF16),
             pltpu.VMEM((T, EB), BF16),
             pltpu.VMEM((T, 2 * D), F32),
-            pltpu.VMEM((T, 128), F32),
+            pltpu.VMEM((T, 128), BF16),
             pltpu.VMEM((T, 2 * D), F32),
             pltpu.VMEM((L * CAP, 2 * D), F32),
             pltpu.VMEM((H, 2 * D), F32),
@@ -263,12 +292,9 @@
         + [dma((L,))] * 8
         + [dma((G,))] * 2,
         compiler_params=pltpu.CompilerParams(
-            collective_id=0, has_side_effects=True, vmem_limit_bytes=48 * 2**20
+            collective_id=0, has_side_effects=True, vmem_limit_bytes=64 * 2**20
         ),
-    )(
-        node, hub, edge, src.reshape(-1, 128), dst.reshape(-1, 128), sgn.reshape(-1, 128), rows,
-        w1, b1.reshape(1, -1), w2, b2.reshape(1, -1), w3, b3.reshape(1, -1), w4, b4.reshape(1, -1),
-    )
+    )(*args)
 
 
 def solution(mesh):

time: 40.9 us -> 32.2 us (0.79)
  local copies, waits for them, and re-layouts: 11 us -> 2.28 us
  Pallas kernels: 28.6 us -> 29.1 us
    unnamed x32 -> x4, local copies, waits for them, and re-layouts: 11 us -> 2.28 us
    pallas_call x1, Pallas kernels: 28.6 us -> 29.1 us  [per_device(): pl.pallas_call(functools.partial(kernel, sizes), out_shape=(jax.ShapeDtyp...]
where the time goes in v1:
time: 32.2 us; the launch traced here: 32 us
  Pallas kernels  29.1 us (90%)
  local copies, waits for them, and re-layouts  2.28 us (7%)
  between operations  0.65 us (2%)
    pallas_call x1, Pallas kernels, per_device(): pl.pallas_call(functools.partial(kernel, sizes), out_shape=(jax.ShapeDtyp...  29.1 us
    unnamed x4, local copies, waits for them, and re-layouts  2.28 us

profile of v1, /device:TPU:0, one launch (start us, length us, event | category | flops | bytes accessed | tf_op | source)
XLA Modules:
  0.0 32.0 jit_solution(13977482877337862952)
XLA Ops:
  0.6 29.1 %shard_map.158 = (f32[512,128]{1,0:T(8,128)}, f32[32,128]{1,0:T(8,128)}) custom-call(f32[512,128]{1,0:T(8,128)} %node_h.1, f32[32,128]{1,0:T(8,128)} %hub_h.1, f32[2048,128]{1,0:T(8,128)} %edge_h.1, s32[16,128]{1,0:T(8,128)} %bitcast.7, s32[16,128]{1,0:T(8,128)} %bitcast.8, s32[16,128]{1,0:T(8,128)} %bitcast.9, s32[4,48]{1,0:T(4,128)} %rows_h.1, ...), custom_call_target="tpu_custom_call" | custom-call | tf_op jit(solution)/shard_map/pallas_call | solution.py:263
  29.7 0.0 copy-start
  29.7 1.7 %copy.19 = f32[512,128]{1,0:T(8,128)} copy(f32[512,128]{1,0:T(8,128)} %get-tuple-element.4) | data formatting | bytes 524288
  31.4 0.0 copy-done
  31.4 0.6 %copy.20 = f32[32,128]{1,0:T(8,128)} copy(f32[32,128]{1,0:T(8,128)S(1)} %copy-done) | data formatting | bytes 32768
Async XLA Ops:
  29.7 1.7 %copy-start = (f32[32,128]{1,0:T(8,128)S(1)}, f32[32,128]{1,0:T(8,128)}, u32[]{:S(2)}) copy-start(f32[32,128]{1,0:T(8,128)} %get-tuple-element.5) | copy-start | bytes 49156

commit v2 on v1

--- a/solution.py
+++ b/solution.py
@@ -55,7 +55,7 @@
     node_out, hub_out,
     node, hub, edge, src, dst, sgn, rows, w1, b1, w2, b2, w3, b3, w4, b4, in_sem,
     w1s, w1l, w2p, w3s, w3l, w4p,
-    table, outbuf, mir, hubs, oh_s, oh_d, oh_t, sums, dacc, res, back, huba, hubb, hubsend,
+    table, outbuf, mir, hubs, own_s, own_d, oh_s, oh_d, x_s, x_d, oh_t, sums, dacc, msg, got_msg, hubb, hubsend,
     m_send, m_recv, h_send, h_recv, r_send, r_recv, a_send, a_recv, g_send, g_recv,
 ):
     L, G, V, CAP, H, HS, E, EB, T, TP = sizes
@@ -119,7 +119,34 @@
     mir[part(lane, CAP), :] = outbuf[part(lane, CAP), :]
     hubs[part(lane, HS), :] = hub[...]
 
-    for c in loads[3:]:
+    for c in loads[3:5]:
+        c.wait()
+    NR = EB // 128
+    lane_id = lane_iota.astype(F32).astype(BF16)
+    sub_id = lax.broadcasted_iota(jnp.int32, (128, 128), 0).astype(F32).astype(BF16)
+    one, zero = jnp.ones((128, 128), BF16), jnp.zeros((128, 128), BF16)
+
+    def digits(ids):
+        high = ids >> 7
+        return (ids & 127).astype(F32).astype(BF16), high.astype(F32).astype(BF16)
+
+    def own_block(i, carry):
+        for ids, own, other, found in ((src, own_s, oh_s, x_s), (dst, own_d, oh_d, x_d)):
+            for j in range(NR):
+                low, high = digits(column(ids[pl.ds(i * NR + j, 1), :]))
+                hot = jnp.where(low == lane_id, one, zero)
+                for k in range(TP // 128):
+                    place = jnp.where(high == jnp.asarray(k, BF16), hot, zero)
+                    if 128 * k < V:
+                        own[128 * j : 128 * (j + 1), 128 * k : 128 * (k + 1)] = place
+                    else:
+                        other[part(i * NR + j, 128), 128 * k - V : 128 * (k + 1) - V] = place
+            found[part(i, EB), :] = dot(own[...], table[:V, :]).astype(BF16)
+        return carry
+
+    lax.fori_loop(0, E // EB, own_block, 0)
+
+    for c in loads[5:]:
         c.wait()
     store_weights(w1, w1s, w1l)
     store_out_weights(w2, w2p)
@@ -138,39 +165,22 @@
     table[V + LC : T, :128] = hi
     table[V + LC : T, 128:] = lo
 
-    NR = EB // 128
-    lane_id = lane_iota.astype(F32).astype(BF16)
-    sub_id = lax.broadcasted_iota(jnp.int32, (128, 128), 0).astype(F32).astype(BF16)
-    one, zero = jnp.ones((128, 128), BF16), jnp.zeros((128, 128), BF16)
-
-    def digits(ids):
-        high = ids >> 7
-        return (ids & 127).astype(F32).astype(BF16), high.astype(F32).astype(BF16)
-
     def edge_block(i, carry):
         signs = []
         for j in range(NR):
             at = pl.ds(i * NR + j, 1)
             row = slice(128 * j, 128 * (j + 1))
-            d_row = dst[at, :]
-            s_low, s_high = digits(column(src[at, :]))
-            d_low, d_high = digits(column(d_row))
-            r_low, r_high = digits(jnp.broadcast_to(d_row, (128, 128)))
-            s_hot = jnp.where(s_low == lane_id, one, zero)
-            d_hot = jnp.where(d_low == lane_id, one, zero)
+            r_low, r_high = digits(jnp.broadcast_to(dst[at, :], (128, 128)))
             r_hot = jnp.where(r_low == sub_id, one, zero)
             for k in range(TP // 128):
-                cols = slice(128 * k, 128 * (k + 1))
-                k16 = jnp.asarray(k, BF16)
-                oh_s[row, cols] = jnp.where(s_high == k16, s_hot, zero)
-                oh_d[row, cols] = jnp.where(d_high == k16, d_hot, zero)
                 n = min(128, T - 128 * k)
-                hot = jnp.where(r_high == k16, r_hot, zero)[:n]
+                hot = jnp.where(r_high == jnp.asarray(k, BF16), r_hot, zero)[:n]
                 oh_t[128 * k : 128 * k + n, row] = hot
                 dacc[128 * k : 128 * k + n, :] += hot
             signs.append((2 * column(sgn[at, :]) - 1).astype(F32))
-        xs = dot(oh_s[...], table[...]).astype(BF16)
-        xd = dot(oh_d[...], table[...]).astype(BF16)
+        here = part(i, EB)
+        xs = (x_s[here, :].astype(F32) + dot(oh_s[here, :], table[V:, :])).astype(BF16)
+        xd = (x_d[here, :].astype(F32) + dot(oh_d[here, :], table[V:, :])).astype(BF16)
         eh, el = split(edge[pl.ds(pl.multiple_of(i * EB, EB), EB), :])
         pre = dot(jnp.concatenate([xs, xd, eh, el], axis=1), w1s[...])
         pre = pre + dot(jnp.concatenate([xs[:, :128], xd[:, :128], eh], axis=1), w1l[...])
@@ -182,27 +192,43 @@
 
     lax.fori_loop(0, E // EB, edge_block, 0)
 
-    res[:, :128] = sums[:, :128] + sums[:, 128:]
-    res[:, 128:] = dot(dacc[...], jnp.ones((128, 128), BF16))
-    for p in lanes:
-        c = remote(res.at[part(p, HS, V + LC)], huba.at[part(lane, HS)], a_send.at[p], a_recv.at[lane], group, p)
-        c.start()
-        sends.append(c)
-    for p in lanes:
-        c = remote(res.at[part(p, CAP, V)], back.at[part(lane, CAP)], r_send.at[p], r_recv.at[lane], group, p)
-        c.start()
-        sends.append(c)
-    huba[part(lane, HS), :] = res[part(lane, HS, V + LC), :]
-    back[part(lane, CAP), :] = res[part(lane, CAP, V), :]
-
-    for p in lanes:
-        remote(res.at[part(p, HS)], huba.at[part(p, HS)], a_send.at[p], a_recv.at[p], group, p).wait_recv()
-    total = huba[:HS, :]
+    for p in range(L):
+        hub_at, mir_at = V + LC + p * HS, V + p * CAP
+        msg[p, :HS] = sums[hub_at : hub_at + HS, :128] + sums[hub_at : hub_at + HS, 128:]
+        counts = jnp.concatenate(
+            [dacc[hub_at : hub_at + HS, :], dacc[mir_at : mir_at + CAP, :], zero[: 128 - HS - CAP]], axis=0
+        )
+        msg[p, HS : HS + 8] = lax.dot_general(
+            one[:8], counts, (((1,), (1,)), ((), ())), preferred_element_type=F32
+        )
+        msg[p, HS + 8 :] = sums[mir_at : mir_at + CAP, :128] + sums[mir_at : mir_at + CAP, 128:]
+    first, second = pl.ds(0, HS + 8), pl.ds(HS + 8, CAP)
+    for p in lanes:
+        c = remote(msg.at[p, first], got_msg.at[lane, first], a_send.at[p], a_recv.at[lane], group, p)
+        c.start()
+        sends.append(c)
+    for p in lanes:
+        c = remote(msg.at[p, second], got_msg.at[lane, second], r_send.at[p], r_recv.at[lane], group, p)
+        c.start()
+        sends.append(c)
+    got_msg[lane] = msg[lane]
+
+    def own_part(x):
+        return dot(jnp.concatenate(split(x), axis=1), w3s[:256]) + dot(x.astype(BF16), w3l[:128]) + 0.5 * b3[...]
+
+    node_pre = own_part(node[...])
+    hub_pre = own_part(hub[...])
+    own_sum = sums[:V, :128] + sums[:V, 128:]
+    own_deg = dot(dacc[:V, :], one)
+    v_iota = lax.broadcasted_iota(jnp.int32, (V, LC), 0)
+    back_hot = jnp.where(v_iota == flat_rows[:, :LC], 1.0, 0.0).astype(BF16)
+
+    for p in lanes:
+        remote(msg.at[p, first], got_msg.at[p, first], a_send.at[p], a_recv.at[p], group, p).wait_recv()
+    total = got_msg[0, : HS + 8]
     for p in range(1, L):
-        total = total + huba[HS * p : HS * (p + 1), :]
-    deg = jnp.concatenate([total[:, 128:], jnp.zeros((128 - HS, 128), F32)], axis=0)
-    hubsend[:HS, :] = total[:, :128]
-    hubsend[HS:, :] = jnp.transpose(deg)[:8, :]
+        total = total + got_msg[p, : HS + 8]
+    hubsend[...] = total
     for q in groups:
         c = remote(hubsend, hubb.at[group], g_send.at[q], g_recv.at[group], q, lane)
         c.start()
@@ -210,25 +236,24 @@
     hubb[group] = hubsend[...]
 
     for p in lanes:
-        remote(res.at[part(p, CAP)], back.at[part(p, CAP)], r_send.at[p], r_recv.at[p], group, p).wait_recv()
-    v_iota = lax.broadcasted_iota(jnp.int32, (V, LC), 0)
-    back_hot = jnp.where(v_iota == flat_rows[:, :LC], 1.0, 0.0).astype(BF16)
-    sh, sl = split(back[:, :128])
-    dh, dl = split(back[:, 128:])
+        remote(msg.at[p, second], got_msg.at[p, second], r_send.at[p], r_recv.at[p], group, p).wait_recv()
+    sh, sl = split(jnp.concatenate([got_msg[p, HS + 8 :] for p in range(L)], axis=0))
+    dh, dl = split(
+        jnp.concatenate([column(got_msg[p, HS : HS + 1])[HS : HS + CAP] for p in range(L)], axis=0)
+    )
     got = dot(back_hot, jnp.concatenate([sh, sl], axis=1))
     got_deg = dot(back_hot, jnp.concatenate([dh, dl], axis=1))
 
-    def update(x, summed, degree):
-        xh, xl = split(x)
+    def update(x, pre, summed, degree):
         mh, ml = split(summed / jnp.maximum(degree, 1.0))
-        pre = dot(jnp.concatenate([xh, xl, mh, ml], axis=1), w3s[...])
-        pre = pre + dot(jnp.concatenate([xh, mh], axis=1), w3l[...])
-        return x + out_layer(silu(pre + 0.5 * b3[...]), w4p) + b4[...]
+        pre = pre + dot(jnp.concatenate([mh, ml], axis=1), w3s[256:]) + dot(mh, w3l[128:])
+        return x + out_layer(silu(pre), w4p) + b4[...]
 
     node_out[...] = update(
         node[...],
-        res[:V, :128] + got[:, :128] + got[:, 128:],
-        res[:V, 128:] + got_deg[:, :128] + got_deg[:, 128:],
+        node_pre,
+        own_sum + got[:, :128] + got[:, 128:],
+        own_deg + got_deg[:, :128] + got_deg[:, 128:],
     )
 
     for q in groups:
@@ -236,7 +261,7 @@
     whole = hubb[0]
     for q in range(1, G):
         whole = whole + hubb[q]
-    hub_out[...] = update(hub[...], whole[:HS, :], column(whole[HS : HS + 1, :])[:HS])
+    hub_out[...] = update(hub[...], hub_pre, whole[:HS, :], column(whole[HS : HS + 1, :])[:HS])
     for c in sends:
         c.wait_send()
 
@@ -253,7 +278,7 @@
     T = V + L * CAP + H
     TP = -(-T // 128) * 128
     sizes = (L, G, V, CAP, H, HS, E, EB, T, TP)
-    assert E <= 256 * 128
+    assert E <= 256 * 128 and HS + CAP <= 128 and V % 128 == 0
     dma = pltpu.SemaphoreType.DMA
     vmem = pl.BlockSpec(memory_space=pltpu.VMEM)
     args = (
@@ -278,14 +303,17 @@
             pltpu.VMEM((L * CAP, D), F32),
             pltpu.VMEM((L * CAP, D), F32),
             pltpu.VMEM((H, D), F32),
-            pltpu.VMEM((EB, TP), BF16),
-            pltpu.VMEM((EB, TP), BF16),
+            pltpu.VMEM((EB, V), BF16),
+            pltpu.VMEM((EB, V), BF16),
+            pltpu.VMEM((E, TP - V), BF16),
+            pltpu.VMEM((E, TP - V), BF16),
+            pltpu.VMEM((E, 2 * D), BF16),
+            pltpu.VMEM((E, 2 * D), BF16),
             pltpu.VMEM((T, EB), BF16),
             pltpu.VMEM((T, 2 * D), F32),
             pltpu.VMEM((T, 128), BF16),
-            pltpu.VMEM((T, 2 * D), F32),
-            pltpu.VMEM((L * CAP, 2 * D), F32),
-            pltpu.VMEM((H, 2 * D), F32),
+            pltpu.VMEM((L, HS + 8 + CAP, D), F32),
+            pltpu.VMEM((L, HS + 8 + CAP, D), F32),
             pltpu.VMEM((G, HS + 8, D), F32),
             pltpu.VMEM((HS + 8, D), F32),
         ]

time: 32.2 us -> 29.2 us (0.907)
  Pallas kernels: 29.1 us -> 26.1 us
    pallas_call x1, Pallas kernels: 29.1 us -> 26.1 us  [per_device(): pl.pallas_call(functools.partial(kernel, sizes), out_shape=(jax.ShapeDtyp...]
where the time goes in v2:
time: 29.2 us; the launch traced here: 29 us
  Pallas kernels  26.1 us (89%)
  local copies, waits for them, and re-layouts  2.28 us (8%)
  between operations  0.65 us (2%)
    pallas_call x1, Pallas kernels, per_device(): pl.pallas_call(functools.partial(kernel, sizes), out_shape=(jax.ShapeDtyp...  26.1 us
    unnamed x4, local copies, waits for them, and re-layouts  2.28 us

profile of v2, /device:TPU:0, one launch (start us, length us, event | category | flops | bytes accessed | tf_op | source)
XLA Modules:
  0.0 29.0 jit_solution(10526597005594235239)
XLA Ops:
  0.6 26.1 %shard_map.158 = (f32[512,128]{1,0:T(8,128)}, f32[32,128]{1,0:T(8,128)}) custom-call(f32[512,128]{1,0:T(8,128)} %node_h.1, f32[32,128]{1,0:T(8,128)} %hub_h.1, f32[2048,128]{1,0:T(8,128)} %edge_h.1, s32[16,128]{1,0:T(8,128)} %bitcast.7, s32[16,128]{1,0:T(8,128)} %bitcast.8, s32[16,128]{1,0:T(8,128)} %bitcast.9, s32[4,48]{1,0:T(4,128)} %rows_h.1, ...), custom_call_target="tpu_custom_call" | custom-call | tf_op jit(solution)/shard_map/pallas_call | solution.py:288
  26.7 0.0 copy-start
  26.7 1.7 %copy.19 = f32[512,128]{1,0:T(8,128)} copy(f32[512,128]{1,0:T(8,128)} %get-tuple-element.4) | data formatting | bytes 524288
  28.4 0.0 copy-done
  28.4 0.6 %copy.20 = f32[32,128]{1,0:T(8,128)} copy(f32[32,128]{1,0:T(8,128)S(1)} %copy-done) | data formatting | bytes 32768
Async XLA Ops:
  26.7 1.7 %copy-start = (f32[32,128]{1,0:T(8,128)S(1)}, f32[32,128]{1,0:T(8,128)}, u32[]{:S(2)}) copy-start(f32[32,128]{1,0:T(8,128)} %get-tuple-element.5) | copy-start | bytes 49156

commit v3 on v2

--- a/solution.py
+++ b/solution.py
@@ -201,12 +201,14 @@
         msg[p, HS : HS + 8] = lax.dot_general(
             one[:8], counts, (((1,), (1,)), ((), ())), preferred_element_type=F32
         )
+    first, second = pl.ds(0, HS + 8), pl.ds(HS + 8, CAP)
+    for p in lanes:
+        c = remote(msg.at[p, first], got_msg.at[lane, first], a_send.at[p], a_recv.at[lane], group, p)
+        c.start()
+        sends.append(c)
+    for p in range(L):
+        mir_at = V + p * CAP
         msg[p, HS + 8 :] = sums[mir_at : mir_at + CAP, :128] + sums[mir_at : mir_at + CAP, 128:]
-    first, second = pl.ds(0, HS + 8), pl.ds(HS + 8, CAP)
-    for p in lanes:
-        c = remote(msg.at[p, first], got_msg.at[lane, first], a_send.at[p], a_recv.at[lane], group, p)
-        c.start()
-        sends.append(c)
     for p in lanes:
         c = remote(msg.at[p, second], got_msg.at[lane, second], r_send.at[p], r_recv.at[lane], group, p)
         c.start()
@@ -287,7 +289,7 @@
     )
     return pl.pallas_call(
         functools.partial(kernel, sizes),
-        out_shape=(jax.ShapeDtypeStruct((V, D), F32), jax.ShapeDtypeStruct((HS, D), F32)),
+        out_shape=(pltpu.VMEM((V, D), F32), pltpu.VMEM((HS, D), F32)),
         in_specs=[pl.BlockSpec(memory_space=pltpu.HBM)] * 15,
         out_specs=(vmem, vmem),
         scratch_shapes=[pltpu.VMEM(a.shape, a.dtype) for a in args]
@@ -320,7 +322,7 @@
         + [dma((L,))] * 8
         + [dma((G,))] * 2,
         compiler_params=pltpu.CompilerParams(
-            collective_id=0, has_side_effects=True, vmem_limit_bytes=64 * 2**20
+            collective_id=0, has_side_effects=True, vmem_limit_bytes=63 * 2**20
         ),
     )(*args)
 

time: 29.2 us -> 27.5 us (0.942)
  local copies, waits for them, and re-layouts: 2.28 us -> 1.31 us
  Pallas kernels: 26.1 us -> 25.4 us
    unnamed x4 -> x2, local copies, waits for them, and re-layouts: 2.28 us -> 1.31 us
    pallas_call x1, Pallas kernels: 26.1 us -> 25.4 us  [per_device(): pl.pallas_call(functools.partial(kernel, sizes), out_shape=(pltpu.VMEM((V...]
where the time goes in v3:
time: 27.5 us; the launch traced here: 27.3 us
  Pallas kernels  25.4 us (92%)
  local copies, waits for them, and re-layouts  1.31 us (5%)
  between operations  0.64 us (2%)
    pallas_call x1, Pallas kernels, per_device(): pl.pallas_call(functools.partial(kernel, sizes), out_shape=(pltpu.VMEM((V...  25.4 us
    unnamed x2, local copies, waits for them, and re-layouts  1.31 us

profile of v3, /device:TPU:0, one launch (start us, length us, event | category | flops | bytes accessed | tf_op | source)
XLA Modules:
  0.0 27.3 jit_solution(4203826790085015746)
XLA Ops:
  0.6 25.4 %shard_map.158 = (f32[512,128]{1,0:T(8,128)S(1)}, f32[32,128]{1,0:T(8,128)S(1)}) custom-call(f32[512,128]{1,0:T(8,128)} %node_h.1, f32[32,128]{1,0:T(8,128)} %hub_h.1, f32[2048,128]{1,0:T(8,128)} %edge_h.1, s32[16,128]{1,0:T(8,128)} %bitcast.7, s32[16,128]{1,0:T(8,128)} %bitcast.8, s32[16,128]{1,0:T(8,128)} %bitcast.9, s32[4,48]{1,0:T(4,128)} %rows_h.1, ...), custom_call_target="tpu_custom_call" | custom-call | tf_op jit(solution)/shard_map/pallas_call | solution.py:290
  26.0 0.7 %copy.19 = f32[512,128]{1,0:T(8,128)} copy(f32[512,128]{1,0:T(8,128)S(1)} %get-tuple-element.2) | data formatting | bytes 524288
  26.7 0.6 %copy.20 = f32[32,128]{1,0:T(8,128)} copy(f32[32,128]{1,0:T(8,128)S(1)} %get-tuple-element.3) | data formatting | bytes 32768
